TPU v7x, 32 devices: a whole 2x2x4 slice. The times are simulated.
32 devices in a mesh: row: 4 (over y, core), col: 8 (over z, x).
Axes of the slice: x: 2, y: 2, z: 4, core: 2. Of those that a mesh axis runs over, the one named last changes fastest.
Arguments:
- user_factors: bfloat16 [16384, 64], P(('row', 'col')), may hold values from -4 to 4
- item_factors: bfloat16 [16384, 64], P(('col', 'row')), may hold values from -4 to 4
- start_vectors: bfloat16 [16384, 128], P(('col', 'row')), may hold values from -6 to 6
- ratings: bfloat16 [4, 8, 96, 128, 128], P('row', 'col'), may hold values from -6 to 6
- tile_rows: int32 [4, 8, 96], P('row', 'col'), may hold values from 0 to 31, as said below
- tile_cols: int32 [4, 8, 96], P('row', 'col'), may hold values from 0 to 15, as said below
- tile_count: int32 [4, 8], P('row', 'col'), may hold values from 32 to 96, as said below
Outputs:
- user_basis_out: float32 [16384, 128], P(('row', 'col'))
- item_basis_out: float32 [16384, 128], P(('col', 'row'))
Inputs may be any that keep to these rules, and one draw needn't show every extreme that they name: `tile_rows`: within one device the slots name distinct tiles of its blocks. `tile_cols`: within one device the slots name distinct tiles of its blocks. `tile_count`: some device uses all 96 slots in every draw; slots at or past a device's count are unused.
All inputs are finite; a program needn't handle non-finite values.
Results may differ from a plain program's by a relative error of at most 0.009.
Values may be sent and summed in bfloat16 or wider, within the bound.
A program may use at most 64 MiB of HBM per device.

v0:
```python
import jax
import jax.numpy as jnp
from jax import lax
from jax.sharding import PartitionSpec as P


def gram_of(block):
    return jnp.dot(
        block.T, block, precision=lax.Precision.HIGHEST, preferred_element_type=jnp.float32
    )


def solve_with(block, gram):
    lower = jnp.linalg.cholesky(gram)
    return lax.linalg.triangular_solve(lower, block, left_side=False, lower=True, transpose_a=True)


def shards(user_factors, item_factors, start_vectors, ratings, tile_rows, tile_cols, tile_count):
    tile = ratings.shape[-1]
    slots_total = ratings.shape[2]
    rank = user_factors.shape[1]
    user_block = lax.all_gather(user_factors, "col", axis=0, tiled=True)
    item_block, item_basis = (
        lax.all_gather(item_factors, "row", axis=0, tiled=True),
        lax.all_gather(start_vectors, "row", axis=0, tiled=True),
    )
    user_tiles = user_block.shape[0] // tile
    item_tiles = item_block.shape[0] // tile
    rows = tile_rows[0, 0]
    cols = tile_cols[0, 0]
    valid = (jnp.arange(slots_total, dtype=jnp.int32) < tile_count[0, 0]).astype(jnp.float32)
    left = user_block.reshape(user_tiles, tile, rank)[rows]
    right = item_block.reshape(item_tiles, tile, rank)[cols]
    product = jnp.einsum("kir,kjr->kij", left, right, preferred_element_type=jnp.float32)
    residual = ((product - ratings[0, 0].astype(jnp.float32)) * valid[:, None, None]).astype(
        jnp.bfloat16
    )
    users_share = user_factors.shape[0]
    items_share = item_factors.shape[0]
    users_total = users_share * lax.axis_size("row") * lax.axis_size("col")
    items_total = items_share * lax.axis_size("row") * lax.axis_size("col")
    for step_index in range(2):
        forward_picked = item_basis.reshape(item_tiles, tile, item_basis.shape[1])[cols]
        forward_contrib = jnp.einsum(
            "kij,kjc->kic", residual, forward_picked, preferred_element_type=jnp.float32
        )
        forward_summed = jax.ops.segment_sum(forward_contrib, rows, num_segments=user_tiles)
        partial_value = forward_summed.reshape(user_tiles * tile, item_basis.shape[1])
        share_sum = lax.psum_scatter(partial_value, "col", scatter_dimension=0, tiled=True)
        gram = lax.psum(gram_of(share_sum), ("row", "col"))
        user_share = solve_with(share_sum, gram)
        user_basis = lax.all_gather(user_share.astype(jnp.bfloat16), "col", axis=0, tiled=True)
        picked = user_basis.reshape(user_tiles, tile, user_basis.shape[1])[rows]
        contrib = jnp.einsum("kij,kic->kjc", residual, picked, preferred_element_type=jnp.float32)
        summed = jax.ops.segment_sum(contrib, cols, num_segments=item_tiles)
        partial_items = summed.reshape(item_tiles * tile, user_basis.shape[1])
        share_items = lax.psum_scatter(partial_items, "row", scatter_dimension=0, tiled=True)
        gram_items = lax.psum(gram_of(share_items), ("row", "col"))
        item_share = solve_with(share_items, gram_items)
        if step_index == 0:
            item_basis = lax.all_gather(item_share.astype(jnp.bfloat16), "row", axis=0, tiled=True)
    user_out = user_share * jnp.sqrt(jnp.float32(users_total))
    item_out = item_share * jnp.sqrt(jnp.float32(items_total))
    return (user_out, item_out)


def solution(mesh):
    in_specs = (
        P(("row", "col"), None),
        P(("col", "row"), None),
        P(("col", "row"), None),
        P("row", "col", None, None, None),
        P("row", "col", None),
        P("row", "col", None),
        P("row", "col"),
    )
    out_specs = (P(("row", "col"), None), P(("col", "row"), None))
    return jax.shard_map(shards, mesh=mesh, in_specs=in_specs, out_specs=out_specs, check_vma=False)
```

profile of v0, /device:TPU:0, one launch (start us, length us, event | category | flops | bytes accessed | tf_op | source)
XLA Modules:
  0.0 1066.7 jit_solution(6509903463113721656)
XLA Ops:
  7.9 33.2 %all_gather.18 = bf16[4096,64]{0,1:T(8,128)(2,1)S(1)} all-gather(bf16[512,64]{0,1:T(8,128)(2,1)} %param.10), channel_id=1, replica_groups=mesh['row'=4,'col'=8] {'col'}, dimensions={0}, use_global_device_ids=true | all-gather | bytes 589824 | tf_op jit(solution)/shard_map/all_gather | solution.py:22
  41.9 6.0 all_gather.19
  48.6 7.5 all_gather.20
  56.1 1.9 gather_fusion.1
  58.1 2.7 gather_fusion.2
  60.8 2.0 gather_fusion
  62.8 4.6 fusion.1
  67.4 3.6 fusion.24
  71.0 1.6 broadcast.82.clone
  72.6 19.9 %scatter_fusion = f32[32,128,128]{2,1,0:T(8,128)} fusion(f32[32,128,128]{2,1,0:T(8,128)} %broadcast.82.clone, s32[96]{0:T(128)S(1)} %bitcast.115, f32[96,128,128]{2,1,0:T(8,128)} %fusion.24), kind=kCustom, calls=%fused_computation.6 | custom fusion | flops 1572864 | bytes 18874752 | tf_op jit(solution)/shard_map/scatter-add | solution.py:47
  92.6 69.5 %reduce-scatter.5.cloned.1.call-done = f32[512,128]{1,0:T(8,128)} async-done(((f32[4096,128]{1,0:T(8,128)}), f32[512,128]{1,0:T(8,128)}) %reduce-scatter.5.cloned.1.call-update) | async-done | bytes 262160 | tf_op jit(solution)/shard_map/reduce_scatter | solution.py:49
  162.1 2.2 fusion.25
  164.6 120.3 %all-reduce.5.cloned.1.call-done = f32[128,128]{0,1:T(8,128)} async-done(((f32[128,128]{0,1:T(8,128)}), f32[128,128]{0,1:T(8,128)}) %all-reduce.5.cloned.1.call-update) | async-done | bytes 65552 | tf_op jit(solution)/shard_map/psum | solution.py:50
  286.6 11.7 %cholesky.74 = f32[128,128]{1,0:T(8,128)S(1)} custom-call(f32[128,128]{1,0:T(8,128)S(1)} %fusion.16), custom_call_target="Cholesky" | custom-call | tf_op jit(solution)/shard_map/jit(cholesky)/cholesky | solution.py:14
  299.7 9.8 custom-call.8
  309.5 2.0 fusion.3
  311.6 40.4 %all-gather.3.cloned.1.call-done = bf16[4096,128]{0,1:T(8,128)(2,1)} async-done(((bf16[512,128]{0,1:T(8,128)(2,1)}), bf16[4096,128]{0,1:T(8,128)(2,1)}) %all-gather.3.cloned.1.call-update) | async-done | bytes 1048592 | tf_op jit(solution)/shard_map/all_gather | solution.py:52
  352.1 2.3 copy.59
  354.3 4.0 gather_fusion.3
  358.3 5.8 fusion.26
  365.2 19.7 %scatter_fusion.1 = f32[16,128,128]{2,1,0:T(8,128)} fusion(f32[16,128,128]{2,1,0:T(8,128)} %broadcast.86.clone, s32[96]{0:T(128)S(1)} %bitcast.117, f32[96,128,128]{2,1,0:T(8,128)} %fusion.26), kind=kCustom, calls=%fused_computation.7 | custom fusion | flops 1572864 | bytes 18874752 | tf_op jit(solution)/shard_map/scatter-add | solution.py:55
  385.0 23.9 %reduce-scatter.7.cloned.1.call-done = f32[512,128]{1,0:T(8,128)} async-done(((f32[2048,128]{1,0:T(8,128)}), f32[512,128]{1,0:T(8,128)}) %reduce-scatter.7.cloned.1.call-update) | async-done | bytes 262160 | tf_op jit(solution)/shard_map/reduce_scatter | solution.py:57
  408.9 2.2 fusion.27
  411.5 121.9 %all-reduce.7.cloned.1.call-done = f32[128,128]{0,1:T(8,128)} async-done(((f32[128,128]{0,1:T(8,128)}), f32[128,128]{0,1:T(8,128)}) %all-reduce.7.cloned.1.call-update) | async-done | bytes 65552 | tf_op jit(solution)/shard_map/psum | solution.py:58
  535.2 11.7 %cholesky.85 = f32[128,128]{1,0:T(8,128)S(1)} custom-call(f32[128,128]{1,0:T(8,128)S(1)} %fusion.14), custom_call_target="Cholesky" | custom-call | tf_op jit(solution)/shard_map/jit(cholesky)/cholesky | solution.py:14
  548.2 9.8 custom-call.9
  559.4 9.0 all_gather.22
  568.4 2.0 copy.60
  570.5 3.8 gather_fusion.4
  574.2 5.5 fusion.28
  579.8 1.6 broadcast.82
  581.4 19.9 %scatter_fusion.2 = f32[32,128,128]{2,1,0:T(8,128)} fusion(f32[32,128,128]{2,1,0:T(8,128)} %broadcast.82, s32[96]{0:T(128)S(1)} %bitcast.116, f32[96,128,128]{2,1,0:T(8,128)} %fusion.28), kind=kCustom, calls=%fused_computation.8 | custom fusion | flops 1572864 | bytes 18874752 | tf_op jit(solution)/shard_map/scatter-add | solution.py:47
  601.3 67.2 %reduce-scatter.9.cloned.1.call-done = f32[512,128]{1,0:T(8,128)} async-done(((f32[4096,128]{1,0:T(8,128)}), f32[512,128]{1,0:T(8,128)}) %reduce-scatter.9.cloned.1.call-update) | async-done | bytes 262160 | tf_op jit(solution)/shard_map/reduce_scatter | solution.py:49
  668.5 2.2 fusion.29
  671.2 120.9 %all-reduce.9.cloned.1.call-done = f32[128,128]{0,1:T(8,128)} async-done(((f32[128,128]{0,1:T(8,128)}), f32[128,128]{0,1:T(8,128)}) %all-reduce.9.cloned.1.call-update) | async-done | bytes 65552 | tf_op jit(solution)/shard_map/psum | solution.py:50
  793.9 11.7 %cholesky.96 = f32[128,128]{1,0:T(8,128)S(1)} custom-call(f32[128,128]{1,0:T(8,128)S(1)} %fusion.12), custom_call_target="Cholesky" | custom-call | tf_op jit(solution)/shard_map/jit(cholesky)/cholesky | solution.py:14
  807.0 9.8 custom-call.10
  816.8 2.0 fusion.23
  818.9 40.4 %all-gather.5.cloned.1.call-done = bf16[4096,128]{0,1:T(8,128)(2,1)} async-done(((bf16[512,128]{0,1:T(8,128)(2,1)}), bf16[4096,128]{0,1:T(8,128)(2,1)}) %all-gather.5.cloned.1.call-update) | async-done | bytes 1048592 | tf_op jit(solution)/shard_map/all_gather | solution.py:52
  859.3 2.3 copy.61
  861.6 4.0 gather_fusion.5
  865.6 5.7 fusion.30
  871.4 12.9 %scatter_fusion.3 = f32[16,128,128]{2,1,0:T(8,128)S(1)} fusion(f32[16,128,128]{2,1,0:T(8,128)S(1)} %broadcast.86, s32[96]{0:T(128)S(1)} %bitcast.118, f32[96,128,128]{2,1,0:T(8,128)} %fusion.30), kind=kCustom, calls=%fused_computation.9 | custom fusion | flops 1572864 | bytes 18874752 | tf_op jit(solution)/shard_map/scatter-add | solution.py:55
  885.6 23.7 %reduce-scatter.11.cloned.1.call-done = f32[512,128]{1,0:T(8,128)} async-done(((f32[2048,128]{1,0:T(8,128)}), f32[512,128]{1,0:T(8,128)}) %reduce-scatter.11.cloned.1.call-update) | async-done | bytes 262160 | tf_op jit(solution)/shard_map/reduce_scatter | solution.py:57
  909.3 2.2 fusion.31
  912.4 120.4 %all-reduce.11.cloned.1.call-done = f32[128,128]{0,1:T(8,128)} async-done(((f32[128,128]{0,1:T(8,128)}), f32[128,128]{0,1:T(8,128)}) %all-reduce.11.cloned.1.call-update) | async-done | bytes 65552 | tf_op jit(solution)/shard_map/psum | solution.py:58
  1034.6 11.7 %cholesky.107 = f32[128,128]{1,0:T(8,128)S(1)} custom-call(f32[128,128]{1,0:T(8,128)S(1)} %fusion.10), custom_call_target="Cholesky" | custom-call | tf_op jit(solution)/shard_map/jit(cholesky)/cholesky | solution.py:14
  1047.7 9.8 custom-call.11
  (61 shorter events, 22.2 us)
Async XLA Ops:
  7.2 154.9 %reduce-scatter.5.cloned.1.call-start = ((), (), s32[]{:S(2)}) async-start(), calls=%async_computation.4 | async-start | bytes 2359296 | tf_op jit(solution)/shard_map/reduce_scatter | solution.py:49
  62.8 4.6 copy-start.1
  67.4 5.2 copy-start.2
  92.5 192.3 %all-reduce.5.cloned.1.call-start = ((), (), s32[]{:S(2)}) async-start(), calls=%async_computation.5 | async-start | bytes 131072 | tf_op jit(solution)/shard_map/psum | solution.py:50
  164.3 187.7 %all-gather.3.cloned.1.call-start = ((), (), s32[]{:S(2)}) async-start(), calls=%async_computation.6 | async-start | bytes 1179648 | tf_op jit(solution)/shard_map/all_gather | solution.py:52
  311.6 97.4 %reduce-scatter.7.cloned.1.call-start = ((), (), s32[]{:S(2)}) async-start(), calls=%async_computation.7 | async-start | bytes 1310720 | tf_op jit(solution)/shard_map/reduce_scatter | solution.py:57
  358.3 6.9 copy-start.3
  384.9 148.4 %all-reduce.7.cloned.1.call-start = ((), (), s32[]{:S(2)}) async-start(), calls=%async_computation.8 | async-start | bytes 131072 | tf_op jit(solution)/shard_map/psum | solution.py:58
  411.2 257.3 %reduce-scatter.9.cloned.1.call-start = ((), (), s32[]{:S(2)}) async-start(), calls=%async_computation.9 | async-start | bytes 2359296 | tf_op jit(solution)/shard_map/reduce_scatter | solution.py:49
  601.2 190.9 %all-reduce.9.cloned.1.call-start = ((), (), s32[]{:S(2)}) async-start(), calls=%async_computation.10 | async-start | bytes 131072 | tf_op jit(solution)/shard_map/psum | solution.py:50
  670.8 188.6 %all-gather.5.cloned.1.call-start = ((), (), s32[]{:S(2)}) async-start(), calls=%async_computation.11 | async-start | bytes 1179648 | tf_op jit(solution)/shard_map/all_gather | solution.py:52
  818.8 90.5 %reduce-scatter.11.cloned.1.call-start = ((), (), s32[]{:S(2)}) async-start(), calls=%async_computation.12 | async-start | bytes 1310720 | tf_op jit(solution)/shard_map/reduce_scatter | solution.py:57
  884.4 1.0 copy-start
  885.4 147.5 %all-reduce.11.cloned.1.call-start = ((), (), s32[]{:S(2)}) async-start(), calls=%async_computation.13 | async-start | bytes 131072 | tf_op jit(solution)/shard_map/psum | solution.py:58
Sparse Core Ops, SparseCore 0:
  92.6 69.3 reduce-scatter.4
  168.2 116.5 all-reduce.4
  311.7 40.3 all-gather.2
  385.1 23.8 reduce-scatter.6
  415.8 117.4 all-reduce.6
  601.4 67.0 reduce-scatter.8
  675.6 116.4 all-reduce.8
  819.0 40.3 all-gather.4
  885.5 23.7 reduce-scatter.10
  915.3 117.4 all-reduce.10
where the time goes:
time: 1080 us; the launch traced here: 1070 us
  waiting for transfers between devices  749 us (69%)
  other arithmetic  169 us (16%)
  blocking collectives  55.7 us (5%)
  matrix products  41.1 us (4%)
  local copies, waits for them, and re-layouts  35.9 us (3%)
  between operations  15.2 us (1%)
    psum x2, waiting for transfers between devices, shards(): gram_items = lax.psum(gram_of(share_items), ('row', 'col'))  242 us
    psum x2, waiting for transfers between devices, shards(): gram = lax.psum(gram_of(share_sum), ('row', 'col'))  241 us
    reduce_scatter x2, waiting for transfers between devices, shards(): lax.psum_scatter(partial_value, 'col', scatter_dimension=0, tiled=True)  137 us
    all_gather x2, waiting for transfers between devices, shards(): lax.all_gather(user_share.astype(jnp.bfloat16), 'col', axis=0, tiled=True)  80.9 us
    another operation x12, other arithmetic, solve_with(): lower = jnp.linalg.cholesky(gram)  49.6 us
    reduce_scatter x2, waiting for transfers between devices, shards(): lax.psum_scatter(partial_items, 'row', scatter_dimension=0, tiled=True)  47.6 us
    another operation x8, other arithmetic, solve_with(): lax.linalg.triangular_solve(lower, block, left_side=False, lower=True, tr...  41.9 us
    scatter-add x2, other arithmetic, shards(): jax.ops.segment_sum(forward_contrib, rows, num_segments=user_tiles)  39.7 us
  transfers between devices with their start and end apart: 10, of which 10 were waited for; matrix products, arithmetic and copies ran while one was open for 0% of the time, Pallas kernels for 0%

commit v1 on v0

v1 whole, which is shorter than its diff:
```python
import functools

import jax
import jax.numpy as jnp
from jax import lax
from jax.experimental import pallas as pl
from jax.experimental.pallas import tpu as pltpu
from jax.sharding import PartitionSpec as P

MESH = pl.DeviceIdType.MESH
HIGHEST = lax.Precision.HIGHEST
ITERS = 2
UNROLL = 4


def aligned(index, size):
    return pl.ds(pl.multiple_of(index * size, size), size)


class Group:
    def __init__(self, axis, size, other_axis):
        self.axis = axis
        self.size = size
        self.outer = size // 2
        self.me = lax.axis_index(axis)
        self.other = lax.axis_index(other_axis)
        self.o = self.me // 2
        self.i = self.me % 2

    def device(self, index):
        if self.axis == "col":
            return (self.other, index)
        return (index, self.other)

    def ahead(self, t):
        return (self.o + t) % self.outer

    def behind(self, t):
        return (self.o + self.outer - t) % self.outer


def remote(src, dst, send, recv, device):
    return pltpu.make_async_remote_copy(
        src_ref=src, dst_ref=dst, send_sem=send, recv_sem=recv, device_id=device, device_id_type=MESH
    )


class Gather:
    def __init__(self, group, full, sems):
        self.group, self.full = group, full
        self.outer_send, self.outer_recv, self.inner_send, self.inner_recv = sems

    def outer_copy(self, t):
        g = self.group
        block = self.full.at[g.me]
        return remote(
            block, block, self.outer_send.at[t], self.outer_recv.at[t], g.device(g.ahead(t) * 2 + g.i)
        )

    def outer_arrival(self, t):
        g = self.group
        block = self.full.at[g.behind(t) * 2 + g.i]
        return remote(
            block, block, self.outer_send.at[t], self.outer_recv.at[t], g.device(g.ahead(t) * 2 + g.i)
        )

    def inner_copy(self, t):
        g = self.group
        block = self.full.at[g.behind(t) * 2 + g.i]
        return remote(
            block, block, self.inner_send.at[t], self.inner_recv.at[t], g.device(g.o * 2 + 1 - g.i)
        )

    def inner_arrival(self, t):
        g = self.group
        block = self.full.at[g.behind(t) * 2 + 1 - g.i]
        return remote(
            block, block, self.inner_send.at[t], self.inner_recv.at[t], g.device(g.o * 2 + 1 - g.i)
        )

    def start(self):
        for t in range(self.group.outer - 1, 0, -1):
            self.outer_copy(t).start()
        self.inner_copy(0).start()

    def forward(self, t):
        self.outer_arrival(t).wait_recv()
        self.inner_copy(t).start()

    def finish(self):
        for t in range(1, self.group.outer):
            self.forward(t)
        for t in range(self.group.outer):
            self.inner_arrival(t).wait_recv()

    def drain(self):
        for t in range(1, self.group.outer):
            self.outer_copy(t).wait_send()
        for t in range(self.group.outer):
            self.inner_copy(t).wait_send()


class Scatter:
    def __init__(self, group, own, inner_out, inner_in, outer_out, outer_in, sems):
        self.group = group
        self.own, self.inner_out, self.inner_in = own, inner_out, inner_in
        self.outer_out, self.outer_in = outer_out, outer_in
        self.outer_send, self.outer_recv, self.inner_send, self.inner_recv = sems

    def inner_copy(self, t):
        g = self.group
        return remote(
            self.inner_out.at[t],
            self.inner_in.at[t],
            self.inner_send.at[t],
            self.inner_recv.at[t],
            g.device(g.o * 2 + 1 - g.i),
        )

    def outer_copy(self, t):
        g = self.group
        return remote(
            self.outer_out.at[t],
            self.outer_in.at[t],
            self.outer_send.at[t],
            self.outer_recv.at[t],
            g.device(g.ahead(t) * 2 + g.i),
        )

    def products(self, matrix, basis):
        g = self.group
        share = self.own.shape[1]
        chunk = min(share, 256)

        def block(index, store):
            def part(h, _):
                base = pl.multiple_of(index * share + h * chunk, chunk)
                store(
                    h,
                    jnp.dot(
                        matrix[pl.ds(base, chunk), :], basis(), preferred_element_type=jnp.float32
                    ),
                )
                return 0

            lax.fori_loop(0, share // chunk, part, 0)

        def step(s, _):
            t = (s + 1) % g.outer
            there = g.ahead(t)

            def store_out(h, value):
                self.inner_out[t, aligned(h, chunk), :] = value.astype(jnp.bfloat16)

            def store_own(h, value):
                self.own[t, aligned(h, chunk), :] = value

            block(there * 2 + 1 - g.i, store_out)
            self.inner_copy(t).start()
            block(there * 2 + g.i, store_own)
            return 0

        lax.fori_loop(0, g.outer, step, 0)

    def pass_on(self):
        def step(t, _):
            self.inner_copy(t).wait_recv()
            self.outer_out[t] = (self.own[t] + self.inner_in[t].astype(jnp.float32)).astype(
                jnp.bfloat16
            )
            self.outer_copy(t).start()
            return 0

        lax.fori_loop(1, self.group.outer, step, 0)

    def total(self):
        self.inner_copy(0).wait_recv()
        self.own[0] = self.own[0] + self.inner_in[0].astype(jnp.float32)

        def step(t, _):
            self.outer_copy(t).wait_recv()
            self.own[0] = self.own[0] + self.outer_in[t].astype(jnp.float32)
            return 0

        lax.fori_loop(1, self.group.outer, step, 0)

    def drain(self):
        for t in range(1, self.group.outer):
            self.outer_copy(t).wait_send()
        for t in range(self.group.outer):
            self.inner_copy(t).wait_send()


class Gram:
    def __init__(self, row, col, parts, arrived, mine, others, full, sems):
        self.row, self.col = row, col
        self.parts, self.arrived, self.mine, self.others, self.full = parts, arrived, mine, others, full
        self.sems = sems

    def scatter_copy(self, t):
        c = self.col
        there = (c.me + t) % c.size
        return remote(
            self.parts.at[there],
            self.arrived.at[t],
            self.sems[0].at[t],
            self.sems[1].at[t],
            c.device(there),
        )

    def exchange_copy(self, t):
        r = self.row
        return remote(
            self.mine.at[0],
            self.others.at[t],
            self.sems[2].at[t],
            self.sems[3].at[t],
            r.device((r.me + t) % r.size),
        )

    def gather_copy(self, t):
        c = self.col
        return remote(
            self.full.at[c.me],
            self.full.at[c.me],
            self.sems[4].at[t],
            self.sems[5].at[t],
            c.device((c.me + t) % c.size),
        )

    def gather_arrival(self, t):
        c = self.col
        block = self.full.at[(c.me + c.size - t) % c.size]
        return remote(
            block, block, self.sems[4].at[t], self.sems[5].at[t], c.device((c.me + t) % c.size)
        )

    def begin(self, block):
        gram = lax.dot_general(
            block, block, (((0,), (0,)), ((), ())), precision=HIGHEST, preferred_element_type=jnp.float32
        )
        rows = self.parts.shape[1]
        for index in range(self.col.size):
            self.parts[index] = gram[index * rows : (index + 1) * rows, :]
        for t in range(1, self.col.size):
            self.scatter_copy(t).start()

    def exchange(self):
        for t in range(1, self.col.size):
            self.scatter_copy(t).wait_recv()
        total = self.parts[self.col.me]
        for t in range(1, self.col.size):
            total = total + self.arrived[t]
        self.mine[0] = total
        for t in range(1, self.row.size):
            self.exchange_copy(t).start()

    def spread(self):
        for t in range(1, self.row.size):
            self.exchange_copy(t).wait_recv()
        total = self.mine[0]
        for t in range(1, self.row.size):
            total = total + self.others[t]
        self.full[self.col.me] = total
        for t in range(1, self.col.size):
            self.gather_copy(t).start()

    def collect(self, work):
        for t in range(1, self.col.size):
            self.gather_arrival(t).wait_recv()
        rows = self.parts.shape[1]
        for index in range(self.col.size):
            work[index * rows : (index + 1) * rows, :] = self.full[index]

    def drain(self):
        for t in range(1, self.col.size):
            self.scatter_copy(t).wait_send()
            self.gather_copy(t).wait_send()
        for t in range(1, self.row.size):
            self.exchange_copy(t).wait_send()


def eliminate(work):
    size = work.shape[0]
    lanes = lax.broadcasted_iota(jnp.int32, (size, size), 1)
    subs = lax.broadcasted_iota(jnp.int32, (size, size), 0)
    lane_row = lax.broadcasted_iota(jnp.int32, (1, size), 1)

    def step(j, _):
        matrix = work[...]
        row = work[pl.ds(j, 1), :]
        pivot = jnp.sum(jnp.where(lane_row == j, row, 0.0), axis=1, keepdims=True)
        scaled = jnp.where(lane_row == j, 1.0, row) / pivot
        here = lanes == j
        column = jnp.sum(jnp.where(here & (subs > j), matrix, 0.0), axis=1, keepdims=True)
        kept = jnp.where(here & (subs > j), 0.0, matrix)
        work[...] = kept - column * scaled
        return 0

    lax.fori_loop(0, size, step, 0)


def inverse_factor(work):
    size = work.shape[0]
    lanes = lax.broadcasted_iota(jnp.int32, (size, size), 1)
    subs = lax.broadcasted_iota(jnp.int32, (size, size), 0)
    matrix = work[...]
    pivots = jnp.sum(jnp.where(lanes == subs, matrix, 0.0), axis=1, keepdims=True)
    unit = jnp.where(lanes == subs, 1.0, jnp.where(lanes < subs, matrix, 0.0))
    return unit * lax.rsqrt(pivots)


def times_transposed(block, inverse):
    return lax.dot_general(
        block, inverse, (((1,), (1,)), ((), ())), precision=HIGHEST, preferred_element_type=jnp.float32
    )


def kernel(n_row, n_col, *refs):
    refs = list(refs)

    def take(count):
        got = refs[:count]
        del refs[:count]
        return got

    rows, cols, slot_of, users, items, start, ratings = take(7)
    user_out, item_out = take(2)
    user_full, item_full, start_full, user_wide, item_wide, res, res_t, block, block_t, work = take(10)
    row = Group("row", n_row, "col")
    col = Group("col", n_col, "row")
    user_gather = Gather(col, user_full, take(4))
    item_gather = Gather(row, item_full, take(4))
    start_gather = Gather(row, start_full, take(4))
    forward_sums, backward_sums, user_gathers, item_gathers, grams = [], [], [], [], []
    for _ in range(ITERS):
        forward_sums.append(Scatter(col, *take(5), take(4)))
        backward_sums.append(Scatter(row, *take(5), take(4)))
        user_gathers.append(Gather(col, *take(1), take(4)))
    for _ in range(ITERS - 1):
        item_gathers.append(Gather(row, *take(1), take(4)))
    for _ in range(2 * ITERS):
        grams.append(Gram(row, col, *take(5), take(6)))
    assert not refs

    barrier = pltpu.get_barrier_semaphore()
    for group in (row, col):
        for t in range(1, group.size):
            pl.semaphore_signal(
                barrier, inc=1, device_id=group.device((group.me + t) % group.size), device_id_type=MESH
            )
    pl.semaphore_wait(barrier, n_row + n_col - 2)

    user_full[col.me] = users[...]
    user_gather.start()
    item_full[row.me] = items[...]
    item_gather.start()
    start_full[row.me] = start[...]
    start_gather.start()

    slots, tile, _ = ratings.shape
    user_tiles = block.shape[0] // tile
    item_tiles = block.shape[1] // tile
    res[slots] = jnp.zeros((tile, tile), jnp.bfloat16)
    res_t[slots] = jnp.zeros((tile, tile), jnp.bfloat16)

    item_gather.finish()
    user_gather.finish()

    half = users.shape[0]
    rank = users.shape[1] // 2
    piece = min(half, tile)
    low = lax.broadcasted_iota(jnp.int32, (piece, 2 * rank), 1) < rank

    def widen(index, _):
        for side in range(2):
            for base in range(0, half, piece):
                packed = user_full[index, base : base + piece, :].astype(jnp.float32)
                value = jnp.where(low, packed, 0.0) if side == 0 else jnp.where(low, 0.0, packed)
                place = index * 2 * half + side * half + base
                inside = pl.ds(pl.multiple_of(place % tile, piece), piece)
                user_wide[place // tile, inside, :] = value.astype(jnp.bfloat16)
        return 0

    lax.fori_loop(0, n_col, widen, 0)
    per_share = item_full.shape[1] // tile
    for index in range(n_row):
        for q in range(per_share):
            item_wide[index * per_share + q] = item_full[index, q * tile : (q + 1) * tile, :]

    def residual(s, _):
        for u in range(UNROLL):
            k = s * UNROLL + u
            left = user_wide[rows[k]]
            right = item_wide[cols[k]]
            product = lax.dot_general(
                left, right, (((1,), (1,)), ((), ())), preferred_element_type=jnp.float32
            )
            value = product - ratings[k].astype(jnp.float32)
            res[k] = value.astype(jnp.bfloat16)
            res_t[k] = value.T.astype(jnp.bfloat16)
        return 0

    lax.fori_loop(0, slots // UNROLL, residual, 0)

    def lay_row(a, _):
        for b in range(item_tiles):
            block[aligned(a, tile), b * tile : (b + 1) * tile] = res[slot_of[a * item_tiles + b]]
        return 0

    lax.fori_loop(0, user_tiles, lay_row, 0)

    def lay_column(b, _):
        for a in range(user_tiles):
            block_t[aligned(b, tile), a * tile : (a + 1) * tile] = res_t[slot_of[a * item_tiles + b]]
        return 0

    lax.fori_loop(0, item_tiles, lay_column, 0)
    start_gather.finish()

    def normalised(gram, source):
        gram.begin(source[0])
        gram.exchange()
        gram.spread()
        gram.collect(work)
        eliminate(work)
        return times_transposed(source[0], inverse_factor(work))

    def whole(full):
        return lambda: full[...].reshape(full.shape[0] * full.shape[1], full.shape[2])

    items_now = start_full
    for index in range(ITERS):
        sums = forward_sums[index]
        sums.products(block, whole(items_now))
        sums.pass_on()
        sums.total()
        basis = normalised(grams[2 * index], sums.own)
        if index == ITERS - 1:
            user_out[...] = basis
        gather = user_gathers[index]
        gather.full[col.me] = basis.astype(jnp.bfloat16)
        gather.start()
        gather.finish()
        sums = backward_sums[index]
        sums.products(block_t, whole(gather.full))
        sums.pass_on()
        sums.total()
        basis = normalised(grams[2 * index + 1], sums.own)
        if index == ITERS - 1:
            item_out[...] = basis
        else:
            gather = item_gathers[index]
            gather.full[row.me] = basis.astype(jnp.bfloat16)
            gather.start()
            gather.finish()
            items_now = gather.full

    for part in (
        [user_gather, item_gather, start_gather]
        + forward_sums
        + backward_sums
        + user_gathers
        + item_gathers
        + grams
    ):
        part.drain()


def shards(n_row, n_col, user_factors, item_factors, start_vectors, ratings, tile_rows, tile_cols, tile_count):
    slots, tile = ratings.shape[2], ratings.shape[-1]
    vecs = start_vectors.shape[1]
    users_share, rank = user_factors.shape
    items_share = item_factors.shape[0]
    users_block, items_block = users_share * n_col, items_share * n_row
    user_tiles, item_tiles = users_block // tile, items_block // tile
    rows, cols = tile_rows[0, 0], tile_cols[0, 0]
    number = jnp.arange(slots, dtype=jnp.int32)
    names = jnp.where(number < tile_count[0, 0], rows * item_tiles + cols, -1)
    places = jnp.arange(user_tiles * item_tiles, dtype=jnp.int32)
    slot_of = slots + jnp.sum(
        jnp.where(names[None, :] == places[:, None], number[None, :] - slots, 0), axis=1
    )
    half = users_share // 2
    users = jnp.concatenate([user_factors[:half], user_factors[half:]], axis=1)
    items = jnp.concatenate([item_factors, item_factors], axis=1)

    bf16, f32 = jnp.bfloat16, jnp.float32
    dma = pltpu.SemaphoreType.DMA

    def gather_sems(size):
        return [dma((size // 2,))] * 4

    def scatter_scratch(size, share):
        outer = size // 2
        return [
            pltpu.VMEM((outer, share, vecs), f32),
            pltpu.VMEM((outer, share, vecs), bf16),
            pltpu.VMEM((outer, share, vecs), bf16),
            pltpu.VMEM((outer, share, vecs), bf16),
            pltpu.VMEM((outer, share, vecs), bf16),
        ] + gather_sems(size)

    scratch = [
        pltpu.VMEM((n_col, half, 2 * rank), bf16),
        pltpu.VMEM((n_row, items_share, 2 * rank), bf16),
        pltpu.VMEM((n_row, items_share, vecs), bf16),
        pltpu.VMEM((user_tiles, tile, 2 * rank), bf16),
        pltpu.VMEM((item_tiles, tile, 2 * rank), bf16),
        pltpu.VMEM((slots + 1, tile, tile), bf16),
        pltpu.VMEM((slots + 1, tile, tile), bf16),
        pltpu.VMEM((users_block, items_block), bf16),
        pltpu.VMEM((items_block, users_block), bf16),
        pltpu.VMEM((vecs, vecs), f32),
    ]
    scratch += gather_sems(n_col) + gather_sems(n_row) + gather_sems(n_row)
    for _ in range(ITERS):
        scratch += scatter_scratch(n_col, users_share)
        scratch += scatter_scratch(n_row, items_share)
        scratch += [pltpu.VMEM((n_col, users_share, vecs), bf16)] + gather_sems(n_col)
    for _ in range(ITERS - 1):
        scratch += [pltpu.VMEM((n_row, items_share, vecs), bf16)] + gather_sems(n_row)
    for _ in range(2 * ITERS):
        part = vecs // n_col
        scratch += [
            pltpu.VMEM((n_col, part, vecs), f32),
            pltpu.VMEM((n_col, part, vecs), f32),
            pltpu.VMEM((1, part, vecs), f32),
            pltpu.VMEM((n_row, part, vecs), f32),
            pltpu.VMEM((n_col, part, vecs), f32),
        ]
        scratch += [dma((n_col,)), dma((n_col,)), dma((n_row,)), dma((n_row,)), dma((n_col,)), dma((n_col,))]

    smem, vmem = pl.BlockSpec(memory_space=pltpu.SMEM), pl.BlockSpec(memory_space=pltpu.VMEM)
    user_basis, item_basis = pl.pallas_call(
        functools.partial(kernel, n_row, n_col),
        out_shape=(
            jax.ShapeDtypeStruct((users_share, vecs), f32),
            jax.ShapeDtypeStruct((items_share, vecs), f32),
        ),
        in_specs=[smem] * 3 + [vmem] * 4,
        out_specs=(vmem, vmem),
        scratch_shapes=scratch,
        compiler_params=pltpu.CompilerParams(
            collective_id=0, has_side_effects=True, vmem_limit_bytes=62 * 1024 * 1024
        ),
    )(rows, cols, slot_of, users, items, start_vectors, ratings[0, 0])
    users_total = users_share * n_row * n_col
    items_total = items_share * n_row * n_col
    return (
        user_basis * jnp.sqrt(jnp.float32(users_total)),
        item_basis * jnp.sqrt(jnp.float32(items_total)),
    )


def solution(mesh):
    in_specs = (
        P(("row", "col"), None),
        P(("col", "row"), None),
        P(("col", "row"), None),
        P("row", "col", None, None, None),
        P("row", "col", None),
        P("row", "col", None),
        P("row", "col"),
    )
    out_specs = (P(("row", "col"), None), P(("col", "row"), None))
    body = functools.partial(shards, mesh.shape["row"], mesh.shape["col"])
    return jax.shard_map(body, mesh=mesh, in_specs=in_specs, out_specs=out_specs, check_vma=False)
```

time: 1080 us -> 255 us (0.24); the launches traced: 1070 us -> 254 us
  waiting for transfers between devices: 749 us -> 0 us
  Pallas kernels: 0 us -> 245 us
  other arithmetic: 169 us -> 6.22 us
  blocking collectives: 55.7 us -> 0 us
  matrix products: 41.1 us -> 0 us
  local copies, waits for them, and re-layouts: 35.9 us -> 1.96 us
  between operations: 15.2 us -> 1.3 us
    psum x4 -> x0, waiting for transfers between devices: 484 us -> none  [the longest x2 242 us: shards(): gram_items = lax.psum(gram_of(share_items), ('row', 'col'))]
    pallas_call x0 -> x1, Pallas kernels: none -> 245 us  [shards(): pl.pallas_call(functools.partial(kernel, n_row, n_col), out_shape=(jax.Sh...]
    reduce_scatter x4 -> x0, waiting for transfers between devices: 184 us -> none  [the longest x2 137 us: shards(): lax.psum_scatter(partial_value, 'col', scatter_dimension=0, tiled=True)]
    another operation x20 -> x0, other arithmetic: 91.4 us -> none  [the longest x12 49.6 us: solve_with(): lower = jnp.linalg.cholesky(gram)]
    all_gather x2 -> x0, waiting for transfers between devices: 80.9 us -> none  [shards(): lax.all_gather(user_share.astype(jnp.bfloat16), 'col', axis=0, tiled=True)]
    scatter-add x4 -> x0, other arithmetic: 72.4 us -> none  [the longest x2 39.7 us: shards(): jax.ops.segment_sum(forward_contrib, rows, num_segments=user_tiles)]
    all_gather x4 -> x0, blocking collectives: 55.7 us -> none  [the longest x1 33.2 us: shards(): user_block = lax.all_gather(user_factors, 'col', axis=0, tiled=True)]
    dot_general x9 -> x0, matrix products: 34.3 us -> none  [the longest x2 11.5 us: shards(): jnp.einsum('kij,kic->kjc', residual, picked, preferred_element_type=jnp.f...]
  transfers between devices with their start and end apart: 10 -> 0, of which waited for: 10 -> 0; matrix products, arithmetic and copies ran while one was open for 0% -> 0% of each run, Pallas kernels for 0% -> 0%
where the time goes in v1:
time: 255 us; the launch traced here: 254 us
  Pallas kernels  245 us (96%)
  other arithmetic  6.22 us (2%)
    pallas_call x1, Pallas kernels, shards(): pl.pallas_call(functools.partial(kernel, n_row, n_col), out_shape=(jax.Sh...  245 us

profile of v1, /device:TPU:0, one launch (start us, length us, event | category | flops | bytes accessed | tf_op | source)
XLA Modules:
  0.0 254.4 jit_solution(13250254514547730464)
XLA Ops:
  1.3 0.7 compare_select_fusion
  2.0 0.1 select_reduce_fusion
  2.1 0.6 broadcast_add_fusion.refs_2_
  2.7 0.8 fusion
  3.4 0.1 copy.17
  3.5 0.1 copy.18
  3.7 0.7 pad_maximum_fusion.1.refs_3_
  4.4 1.0 copy.15
  5.4 0.8 pad_maximum_fusion.refs_4_
  6.1 244.9 %shard_map.86 = (f32[512,128]{1,0:T(8,128)}, f32[512,128]{1,0:T(8,128)}) custom-call(s32[96]{0:T(128)} %bitcast.8, s32[96]{0:T(128)} %bitcast.9, s32[512]{0:T(512)} %broadcast_add_fusion.refs_2_, bf16[256,128]{1,0:T(8,128)(2,1)} %pad_maximum_fusion.1.refs_3_, bf16[512,128]{1,0:T(8,128)(2,1)} %pad_maximum_fusion.refs_4_, bf16[512,128]{1,0:T(8,128)(2,1)} %refs_5_.1, ...), custom_call_target="tpu_custom_call" | custom-call | tf_op jit(solution)/shard_map/pallas_call | solution.py:535
  251.1 1.7 broadcast_multiply_fusion.1
  252.8 1.7 broadcast_multiply_fusion

commit v2 on v1

--- a/solution.py
+++ b/solution.py
@@ -11,6 +11,8 @@
 HIGHEST = lax.Precision.HIGHEST
 ITERS = 2
 UNROLL = 4
+PANEL = 32
+SUB = 8
 
 
 def aligned(index, size):
@@ -280,24 +282,42 @@
             self.exchange_copy(t).wait_send()
 
 
-def eliminate(work):
+def eliminate(work, panel):
     size = work.shape[0]
-    lanes = lax.broadcasted_iota(jnp.int32, (size, size), 1)
-    subs = lax.broadcasted_iota(jnp.int32, (size, size), 0)
-    lane_row = lax.broadcasted_iota(jnp.int32, (1, size), 1)
-
-    def step(j, _):
-        matrix = work[...]
-        row = work[pl.ds(j, 1), :]
-        pivot = jnp.sum(jnp.where(lane_row == j, row, 0.0), axis=1, keepdims=True)
-        scaled = jnp.where(lane_row == j, 1.0, row) / pivot
-        here = lanes == j
-        column = jnp.sum(jnp.where(here & (subs > j), matrix, 0.0), axis=1, keepdims=True)
-        kept = jnp.where(here & (subs > j), 0.0, matrix)
-        work[...] = kept - column * scaled
-        return 0
-
-    lax.fori_loop(0, size, step, 0)
+    base = pl.multiple_of(panel * PANEL, PANEL)
+    lanes = lax.broadcasted_iota(jnp.int32, (PANEL, size), 1)
+    subs = lax.broadcasted_iota(jnp.int32, (PANEL, size), 0)
+    done, active = [], work[pl.ds(base, PANEL), :]
+    for q in range(PANEL // SUB):
+        lane, sub = lanes[q * SUB :], subs[: PANEL - q * SUB]
+        columns = []
+        for b in range(SUB):
+            picked = jnp.where(lane == base + q * SUB + b, active, 0.0)
+            columns.append(jnp.broadcast_to(jnp.sum(picked, axis=1, keepdims=True), active.shape))
+        for a in range(SUB):
+            here = lane == base + q * SUB + a
+            inverse = 1.0 / columns[a][a : a + 1, :]
+            factor = jnp.where(sub > a, columns[a] * inverse, 0.0)
+            row = jnp.where(here[:1], 1.0, active[a : a + 1, :])
+            active = jnp.where(here & (sub > a), 0.0, active) - factor * row
+            for b in range(a + 1, SUB):
+                columns[b] = columns[b] - factor * columns[b][a : a + 1, :]
+        done.append(active[:SUB])
+        active = active[SUB:]
+    rows = jnp.concatenate(done, axis=0)
+    work[pl.ds(base, PANEL), :] = rows
+    diagonal = lanes == base + subs
+    pivots = jnp.sum(jnp.where(diagonal, rows, 0.0), axis=1, keepdims=True)
+    inside = (lanes >= base) & (lanes < base + PANEL)
+    factors = jnp.where(lanes >= base + PANEL, rows, 0.0) / pivots
+    full = jnp.where(inside & (lanes > base + subs), 0.0, jnp.where(diagonal, 1.0, rows))
+    update = lax.dot_general(
+        factors, full, (((0,), (0,)), ((), ())), precision=HIGHEST, preferred_element_type=jnp.float32
+    )
+    lane = lax.broadcasted_iota(jnp.int32, (size, size), 1)
+    sub = lax.broadcasted_iota(jnp.int32, (size, size), 0)
+    fresh = (lane >= base) & (lane < base + PANEL) & (sub >= base + PANEL)
+    work[...] = jnp.where(fresh, 0.0, work[...]) - update
 
 
 def inverse_factor(work):
@@ -423,7 +443,12 @@
         gram.exchange()
         gram.spread()
         gram.collect(work)
-        eliminate(work)
+
+        def panel(index, _):
+            eliminate(work, index)
+            return 0
+
+        lax.fori_loop(0, work.shape[0] // PANEL, panel, 0)
         return times_transposed(source[0], inverse_factor(work))
 
     def whole(full):

time: 255 us -> 221 us (0.87)
  Pallas kernels: 245 us -> 211 us
    pallas_call x1, Pallas kernels: 245 us -> 211 us  [shards(): pl.pallas_call(functools.partial(kernel, n_row, n_col), out_shape=(jax.Sh...]
where the time goes in v2:
time: 221 us; the launch traced here: 220 us
  Pallas kernels  211 us (95%)
  other arithmetic  6.22 us (3%)
    pallas_call x1, Pallas kernels, shards(): pl.pallas_call(functools.partial(kernel, n_row, n_col), out_shape=(jax.Sh...  211 us

profile of v2, /device:TPU:0, one launch (start us, length us, event | category | flops | bytes accessed | tf_op | source)
XLA Modules:
  0.0 220.3 jit_solution(16973867643745021529)
XLA Ops:
  1.3 0.7 compare_select_fusion
  2.0 0.1 select_reduce_fusion
  2.1 0.6 broadcast_add_fusion.refs_2_
  2.7 0.8 fusion
  3.4 0.1 copy.17
  3.5 0.1 copy.18
  3.7 0.7 pad_maximum_fusion.1.refs_3_
  4.4 1.0 copy.15
  5.4 0.8 pad_maximum_fusion.refs_4_
  6.1 210.8 %shard_map.86 = (f32[512,128]{1,0:T(8,128)}, f32[512,128]{1,0:T(8,128)}) custom-call(s32[96]{0:T(128)} %bitcast.8, s32[96]{0:T(128)} %bitcast.9, s32[512]{0:T(512)} %broadcast_add_fusion.refs_2_, bf16[256,128]{1,0:T(8,128)(2,1)} %pad_maximum_fusion.1.refs_3_, bf16[512,128]{1,0:T(8,128)(2,1)} %pad_maximum_fusion.refs_4_, bf16[512,128]{1,0:T(8,128)(2,1)} %refs_5_.1, ...), custom_call_target="tpu_custom_call" | custom-call | tf_op jit(solution)/shard_map/pallas_call | solution.py:560
  216.9 1.7 broadcast_multiply_fusion.1
  218.6 1.7 broadcast_multiply_fusion

commit v3 on v2

--- a/solution.py
+++ b/solution.py
@@ -92,6 +92,9 @@
     def finish(self):
         for t in range(1, self.group.outer):
             self.forward(t)
+        self.arrivals()
+
+    def arrivals(self):
         for t in range(self.group.outer):
             self.inner_arrival(t).wait_recv()
 
@@ -164,13 +167,15 @@
 
         lax.fori_loop(0, g.outer, step, 0)
 
-    def pass_on(self):
+    def pass_on(self, beside=None):
         def step(t, _):
             self.inner_copy(t).wait_recv()
             self.outer_out[t] = (self.own[t] + self.inner_in[t].astype(jnp.float32)).astype(
                 jnp.bfloat16
             )
             self.outer_copy(t).start()
+            if beside is not None:
+                beside(t - 1)
             return 0
 
         lax.fori_loop(1, self.group.outer, step, 0)
@@ -438,48 +443,73 @@
     lax.fori_loop(0, item_tiles, lay_column, 0)
     start_gather.finish()
 
-    def normalised(gram, source):
-        gram.begin(source[0])
-        gram.exchange()
-        gram.spread()
-        gram.collect(work)
-
+    panels = work.shape[0] // PANEL
+
+    def eliminate_from(first):
         def panel(index, _):
             eliminate(work, index)
             return 0
 
-        lax.fori_loop(0, work.shape[0] // PANEL, panel, 0)
-        return times_transposed(source[0], inverse_factor(work))
+        lax.fori_loop(first, panels, panel, 0)
 
     def whole(full):
         return lambda: full[...].reshape(full.shape[0] * full.shape[1], full.shape[2])
 
+    def apply(sums):
+        return times_transposed(sums.own[0], inverse_factor(work))
+
     items_now = start_full
     for index in range(ITERS):
-        sums = forward_sums[index]
+        last = index == ITERS - 1
+        sums, gram, gather = forward_sums[index], grams[2 * index], user_gathers[index]
         sums.products(block, whole(items_now))
-        sums.pass_on()
-        sums.total()
-        basis = normalised(grams[2 * index], sums.own)
-        if index == ITERS - 1:
-            user_out[...] = basis
-        gather = user_gathers[index]
-        gather.full[col.me] = basis.astype(jnp.bfloat16)
+        if index == 0:
+            sums.pass_on()
+            sums.total()
+        else:
+            beside = min(panels, col.outer - 1) if col.outer - 1 <= panels else 0
+            if beside == 0:
+                eliminate_from(0)
+            sums.pass_on((lambda step: eliminate(work, step)) if beside else None)
+            if beside:
+                eliminate_from(beside)
+            sums.total()
+            sums.own[0] = apply(sums)
+        gather.full[col.me] = sums.own[0].astype(jnp.bfloat16)
         gather.start()
-        gather.finish()
-        sums = backward_sums[index]
+        gram.begin(sums.own[0])
+        gram.exchange()
+        gather.forward(1)
+        gram.spread()
+        for t in range(2, col.outer):
+            gather.forward(t)
+        gram.collect(work)
+        eliminate_from(0)
+        if last:
+            user_out[...] = apply(sums)
+        gather.arrivals()
+        sums, gram = backward_sums[index], grams[2 * index + 1]
         sums.products(block_t, whole(gather.full))
         sums.pass_on()
         sums.total()
-        basis = normalised(grams[2 * index + 1], sums.own)
-        if index == ITERS - 1:
-            item_out[...] = basis
+        sums.own[0] = apply(sums)
+        if not last:
+            gather = item_gathers[index]
+            gather.full[row.me] = sums.own[0].astype(jnp.bfloat16)
+            gather.start()
+            gram.begin(sums.own[0])
+            gather.finish()
+            gram.exchange()
+            gram.spread()
+            gram.collect(work)
+            items_now = gather.full
         else:
-            gather = item_gathers[index]
-            gather.full[row.me] = basis.astype(jnp.bfloat16)
-            gather.start()
-            gather.finish()
-            items_now = gather.full
+            gram.begin(sums.own[0])
+            gram.exchange()
+            gram.spread()
+            gram.collect(work)
+            eliminate_from(0)
+            item_out[...] = apply(sums)
 
     for part in (
         [user_gather, item_gather, start_gather]

time: 221 us -> 191 us (0.86)
  Pallas kernels: 211 us -> 181 us
    pallas_call x1, Pallas kernels: 211 us -> 181 us  [shards(): pl.pallas_call(functools.partial(kernel, n_row, n_col), out_shape=(jax.Sh...]
where the time goes in v3:
time: 191 us
  Pallas kernels  181 us (95%)
  other arithmetic  6.22 us (3%)
  local copies, waits for them, and re-layouts  1.96 us (1%)
    pallas_call x1, Pallas kernels, shards(): pl.pallas_call(functools.partial(kernel, n_row, n_col), out_shape=(jax.Sh...  181 us

profile of v3, /device:TPU:0, one launch (start us, length us, event | category | flops | bytes accessed | tf_op | source)
XLA Modules:
  0.0 190.8 jit_solution(1198944462190687544)
XLA Ops:
  1.3 0.7 compare_select_fusion
  2.0 0.1 select_reduce_fusion
  2.1 0.6 broadcast_add_fusion.refs_2_
  2.7 0.8 fusion
  3.4 0.1 copy.17
  3.5 0.1 copy.18
  3.7 0.7 pad_maximum_fusion.1.refs_3_
  4.4 1.0 copy.15
  5.4 0.8 pad_maximum_fusion.refs_4_
  6.1 181.3 %shard_map.86 = (f32[512,128]{1,0:T(8,128)}, f32[512,128]{1,0:T(8,128)}) custom-call(s32[96]{0:T(128)} %bitcast.8, s32[96]{0:T(128)} %bitcast.9, s32[512]{0:T(512)} %broadcast_add_fusion.refs_2_, bf16[256,128]{1,0:T(8,128)(2,1)} %pad_maximum_fusion.1.refs_3_, bf16[512,128]{1,0:T(8,128)(2,1)} %pad_maximum_fusion.refs_4_, bf16[512,128]{1,0:T(8,128)(2,1)} %refs_5_.1, ...), custom_call_target="tpu_custom_call" | custom-call | tf_op jit(solution)/shard_map/pallas_call | solution.py:590
  187.4 1.7 broadcast_multiply_fusion.1
  189.1 1.7 broadcast_multiply_fusion

commit v4 on v3

--- a/solution.py
+++ b/solution.py
@@ -135,7 +135,7 @@
     def products(self, matrix, basis):
         g = self.group
         share = self.own.shape[1]
-        chunk = min(share, 256)
+        chunk = min(share, 512)
 
         def block(index, store):
             def part(h, _):
@@ -167,18 +167,22 @@
 
         lax.fori_loop(0, g.outer, step, 0)
 
-    def pass_on(self, beside=None):
-        def step(t, _):
+    def pass_on(self, beside=()):
+        beside = list(beside)
+
+        def step(t):
             self.inner_copy(t).wait_recv()
             self.outer_out[t] = (self.own[t] + self.inner_in[t].astype(jnp.float32)).astype(
                 jnp.bfloat16
             )
             self.outer_copy(t).start()
-            if beside is not None:
-                beside(t - 1)
-            return 0
-
-        lax.fori_loop(1, self.group.outer, step, 0)
+
+        for t in range(1, self.group.outer):
+            step(t)
+            if beside:
+                beside.pop(0)()
+        for part in beside:
+            part()
 
     def total(self):
         self.inner_copy(0).wait_recv()
@@ -289,7 +293,7 @@
 
 def eliminate(work, panel):
     size = work.shape[0]
-    base = pl.multiple_of(panel * PANEL, PANEL)
+    base = panel * PANEL if isinstance(panel, int) else pl.multiple_of(panel * PANEL, PANEL)
     lanes = lax.broadcasted_iota(jnp.int32, (PANEL, size), 1)
     subs = lax.broadcasted_iota(jnp.int32, (PANEL, size), 0)
     done, active = [], work[pl.ds(base, PANEL), :]
@@ -387,7 +391,6 @@
     user_tiles = block.shape[0] // tile
     item_tiles = block.shape[1] // tile
     res[slots] = jnp.zeros((tile, tile), jnp.bfloat16)
-    res_t[slots] = jnp.zeros((tile, tile), jnp.bfloat16)
 
     item_gather.finish()
     user_gather.finish()
@@ -423,7 +426,6 @@
             )
             value = product - ratings[k].astype(jnp.float32)
             res[k] = value.astype(jnp.bfloat16)
-            res_t[k] = value.T.astype(jnp.bfloat16)
         return 0
 
     lax.fori_loop(0, slots // UNROLL, residual, 0)
@@ -435,12 +437,25 @@
 
     lax.fori_loop(0, user_tiles, lay_row, 0)
 
-    def lay_column(b, _):
-        for a in range(user_tiles):
-            block_t[aligned(b, tile), a * tile : (a + 1) * tile] = res_t[slot_of[a * item_tiles + b]]
-        return 0
-
-    lax.fori_loop(0, item_tiles, lay_column, 0)
+    def transposes():
+        def some(s, _):
+            for u in range(UNROLL):
+                res_t[s * UNROLL + u] = res[s * UNROLL + u].T
+            return 0
+
+        res_t[slots] = jnp.zeros((tile, tile), jnp.bfloat16)
+        lax.fori_loop(0, slots // UNROLL, some, 0)
+
+    def lay_columns(first, end):
+        def lay(b, _):
+            for a in range(user_tiles):
+                block_t[aligned(b, tile), a * tile : (a + 1) * tile] = res_t[
+                    slot_of[a * item_tiles + b]
+                ]
+            return 0
+
+        lax.fori_loop(first, end, lay, 0)
+
     start_gather.finish()
 
     panels = work.shape[0] // PANEL
@@ -464,15 +479,18 @@
         sums, gram, gather = forward_sums[index], grams[2 * index], user_gathers[index]
         sums.products(block, whole(items_now))
         if index == 0:
-            sums.pass_on()
+            middle = item_tiles // 2
+            sums.pass_on(
+                [
+                    transposes,
+                    lambda: lay_columns(0, middle),
+                    lambda: lay_columns(middle, item_tiles),
+                ]
+            )
             sums.total()
         else:
-            beside = min(panels, col.outer - 1) if col.outer - 1 <= panels else 0
-            if beside == 0:
-                eliminate_from(0)
-            sums.pass_on((lambda step: eliminate(work, step)) if beside else None)
-            if beside:
-                eliminate_from(beside)
+            grams[2 * index - 1].collect(work)
+            sums.pass_on([functools.partial(eliminate, work, panel) for panel in range(panels)])
             sums.total()
             sums.own[0] = apply(sums)
         gather.full[col.me] = sums.own[0].astype(jnp.bfloat16)
@@ -501,7 +519,6 @@
             gather.finish()
             gram.exchange()
             gram.spread()
-            gram.collect(work)
             items_now = gather.full
         else:
             gram.begin(sums.own[0])

time: 191 us -> 194 us (1.016)
  Pallas kernels: 181 us -> 184 us
    pallas_call x1, Pallas kernels: 181 us -> 184 us  [shards(): pl.pallas_call(functools.partial(kernel, n_row, n_col), out_shape=(jax.Sh...]
where the time goes in v4:
time: 194 us
  Pallas kernels  184 us (95%)
  other arithmetic  6.22 us (3%)
  local copies, waits for them, and re-layouts  1.96 us (1%)
    pallas_call x1, Pallas kernels, shards(): pl.pallas_call(functools.partial(kernel, n_row, n_col), out_shape=(jax.Sh...  184 us

profile of v4, /device:TPU:0, one launch (start us, length us, event | category | flops | bytes accessed | tf_op | source)
XLA Modules:
  0.0 193.6 jit_solution(18406507160107496990)
XLA Ops:
  1.3 0.7 compare_select_fusion
  2.0 0.1 select_reduce_fusion
  2.1 0.6 broadcast_add_fusion.refs_2_
  2.7 0.8 fusion
  3.4 0.1 copy.17
  3.5 0.1 copy.18
  3.7 0.7 pad_maximum_fusion.1.refs_3_
  4.4 1.0 copy.15
  5.4 0.8 pad_maximum_fusion.refs_4_
  6.1 184.1 %shard_map.86 = (f32[512,128]{1,0:T(8,128)}, f32[512,128]{1,0:T(8,128)}) custom-call(s32[96]{0:T(128)} %bitcast.8, s32[96]{0:T(128)} %bitcast.9, s32[512]{0:T(512)} %broadcast_add_fusion.refs_2_, bf16[256,128]{1,0:T(8,128)(2,1)} %pad_maximum_fusion.1.refs_3_, bf16[512,128]{1,0:T(8,128)(2,1)} %pad_maximum_fusion.refs_4_, bf16[512,128]{1,0:T(8,128)(2,1)} %refs_5_.1, ...), custom_call_target="tpu_custom_call" | custom-call | tf_op jit(solution)/shard_map/pallas_call | solution.py:607
  190.3 1.7 broadcast_multiply_fusion.1
  192.0 1.7 broadcast_multiply_fusion

commit v5 on v4

--- a/solution.py
+++ b/solution.py
@@ -11,6 +11,7 @@
 HIGHEST = lax.Precision.HIGHEST
 ITERS = 2
 UNROLL = 4
+TILE = 128
 PANEL = 32
 SUB = 8
 
@@ -132,37 +133,21 @@
             g.device(g.ahead(t) * 2 + g.i),
         )
 
-    def products(self, matrix, basis):
+    def send_products(self, fetch):
         g = self.group
         share = self.own.shape[1]
-        chunk = min(share, 512)
-
-        def block(index, store):
-            def part(h, _):
-                base = pl.multiple_of(index * share + h * chunk, chunk)
-                store(
-                    h,
-                    jnp.dot(
-                        matrix[pl.ds(base, chunk), :], basis(), preferred_element_type=jnp.float32
-                    ),
-                )
-                return 0
-
-            lax.fori_loop(0, share // chunk, part, 0)
+        per = share // TILE
 
         def step(s, _):
             t = (s + 1) % g.outer
             there = g.ahead(t)
-
-            def store_out(h, value):
-                self.inner_out[t, aligned(h, chunk), :] = value.astype(jnp.bfloat16)
-
-            def store_own(h, value):
-                self.own[t, aligned(h, chunk), :] = value
-
-            block(there * 2 + 1 - g.i, store_out)
+            for q in range(per):
+                place = pl.ds(q * TILE, TILE)
+                tile = fetch((there * 2 + 1 - g.i) * per + q)
+                self.inner_out[t, place, :] = tile.astype(jnp.bfloat16)
             self.inner_copy(t).start()
-            block(there * 2 + g.i, store_own)
+            for q in range(per):
+                self.own[t, pl.ds(q * TILE, TILE), :] = fetch((there * 2 + g.i) * per + q)
             return 0
 
         lax.fori_loop(0, g.outer, step, 0)
@@ -353,9 +338,10 @@
         del refs[:count]
         return got
 
-    rows, cols, slot_of, users, items, start, ratings = take(7)
+    slot_of, row_of, col_of, from_slot, back_row, keep, user_last, item_last = take(8)
+    users, items, start, ratings = take(4)
     user_out, item_out = take(2)
-    user_full, item_full, start_full, user_wide, item_wide, res, res_t, block, block_t, work = take(10)
+    user_full, item_full, start_full, user_wide, item_wide, res, res_t, basis_tiles, sums_of, work = take(10)
     row = Group("row", n_row, "col")
     col = Group("col", n_col, "row")
     user_gather = Gather(col, user_full, take(4))
@@ -388,9 +374,7 @@
     start_gather.start()
 
     slots, tile, _ = ratings.shape
-    user_tiles = block.shape[0] // tile
-    item_tiles = block.shape[1] // tile
-    res[slots] = jnp.zeros((tile, tile), jnp.bfloat16)
+    sums_of[slots] = jnp.zeros(sums_of.shape[1:], jnp.float32)
 
     item_gather.finish()
     user_gather.finish()
@@ -419,42 +403,45 @@
     def residual(s, _):
         for u in range(UNROLL):
             k = s * UNROLL + u
-            left = user_wide[rows[k]]
-            right = item_wide[cols[k]]
+            left = user_wide[row_of[k]]
+            right = item_wide[col_of[k]]
             product = lax.dot_general(
                 left, right, (((1,), (1,)), ((), ())), preferred_element_type=jnp.float32
             )
-            value = product - ratings[k].astype(jnp.float32)
+            value = product - ratings[slot_of[k]].astype(jnp.float32)
             res[k] = value.astype(jnp.bfloat16)
         return 0
 
     lax.fori_loop(0, slots // UNROLL, residual, 0)
 
-    def lay_row(a, _):
-        for b in range(item_tiles):
-            block[aligned(a, tile), b * tile : (b + 1) * tile] = res[slot_of[a * item_tiles + b]]
-        return 0
-
-    lax.fori_loop(0, user_tiles, lay_row, 0)
-
-    def transposes():
+    def transposes(first, end):
         def some(s, _):
             for u in range(UNROLL):
-                res_t[s * UNROLL + u] = res[s * UNROLL + u].T
+                res_t[s * UNROLL + u] = res[from_slot[s * UNROLL + u]].T
             return 0
 
-        res_t[slots] = jnp.zeros((tile, tile), jnp.bfloat16)
-        lax.fori_loop(0, slots // UNROLL, some, 0)
-
-    def lay_columns(first, end):
-        def lay(b, _):
-            for a in range(user_tiles):
-                block_t[aligned(b, tile), a * tile : (a + 1) * tile] = res_t[
-                    slot_of[a * item_tiles + b]
-                ]
+        lax.fori_loop(first, end, some, 0)
+
+    def multiply(matrices, full, pick, way):
+        for index in range(full.shape[0]):
+            per = full.shape[1] // tile
+            for q in range(per):
+                basis_tiles[index * per + q] = full[index, q * tile : (q + 1) * tile, :]
+
+        def some(s, _):
+            total = sums_of[slots + 1]
+            for u in range(2 * UNROLL):
+                k = s * 2 * UNROLL + u
+                part = jnp.dot(
+                    matrices[k], basis_tiles[pick[k]], preferred_element_type=jnp.float32
+                )
+                total = part + keep[way * slots + k] * total
+                sums_of[k] = total
+            sums_of[slots + 1] = total
             return 0
 
-        lax.fori_loop(first, end, lay, 0)
+        sums_of[slots + 1] = jnp.zeros(sums_of.shape[1:], jnp.float32)
+        lax.fori_loop(0, slots // (2 * UNROLL), some, 0)
 
     start_gather.finish()
 
@@ -467,9 +454,6 @@
 
         lax.fori_loop(first, panels, panel, 0)
 
-    def whole(full):
-        return lambda: full[...].reshape(full.shape[0] * full.shape[1], full.shape[2])
-
     def apply(sums):
         return times_transposed(sums.own[0], inverse_factor(work))
 
@@ -477,15 +461,12 @@
     for index in range(ITERS):
         last = index == ITERS - 1
         sums, gram, gather = forward_sums[index], grams[2 * index], user_gathers[index]
-        sums.products(block, whole(items_now))
+        multiply(res, items_now, col_of, 0)
+        sums.send_products(lambda i: sums_of[user_last[i]])
         if index == 0:
-            middle = item_tiles // 2
+            parts = slots // UNROLL // 3
             sums.pass_on(
-                [
-                    transposes,
-                    lambda: lay_columns(0, middle),
-                    lambda: lay_columns(middle, item_tiles),
-                ]
+                [functools.partial(transposes, parts * third, parts * (third + 1)) for third in range(3)]
             )
             sums.total()
         else:
@@ -507,7 +488,8 @@
             user_out[...] = apply(sums)
         gather.arrivals()
         sums, gram = backward_sums[index], grams[2 * index + 1]
-        sums.products(block_t, whole(gather.full))
+        multiply(res_t, gather.full, back_row, 1)
+        sums.send_products(lambda i: sums_of[item_last[i]])
         sums.pass_on()
         sums.total()
         sums.own[0] = apply(sums)
@@ -546,12 +528,36 @@
     items_share = item_factors.shape[0]
     users_block, items_block = users_share * n_col, items_share * n_row
     user_tiles, item_tiles = users_block // tile, items_block // tile
-    rows, cols = tile_rows[0, 0], tile_cols[0, 0]
     number = jnp.arange(slots, dtype=jnp.int32)
-    names = jnp.where(number < tile_count[0, 0], rows * item_tiles + cols, -1)
-    places = jnp.arange(user_tiles * item_tiles, dtype=jnp.int32)
-    slot_of = slots + jnp.sum(
-        jnp.where(names[None, :] == places[:, None], number[None, :] - slots, 0), axis=1
+    places = jnp.stack([tile_rows[0, 0], tile_cols[0, 0]])
+    unused = user_tiles + item_tiles
+    keys = jnp.where(number < tile_count[0, 0], places, unused)
+    ranked = keys * slots + number
+    rank_of = jnp.sum((ranked[:, None, :] < ranked[:, :, None]).astype(jnp.int32), axis=2)
+    chosen = rank_of[:, None, :] == number[None, :, None]
+
+    def pick(way, values):
+        return jnp.sum(jnp.where(chosen[way], values[None, :], 0), axis=1)
+
+    def last_of(way, tiles):
+        target = jnp.arange(tiles, dtype=jnp.int32)[:, None]
+        upto = jnp.sum((keys[way][None, :] <= target).astype(jnp.int32), axis=1)
+        here = jnp.sum((keys[way][None, :] == target).astype(jnp.int32), axis=1)
+        return jnp.where(here > 0, upto - 1, slots)
+
+    def kept(way):
+        earlier = (keys[way][None, :] == keys[way][:, None]) & (number[None, :] < number[:, None])
+        return pick(way, jnp.any(earlier, axis=1).astype(jnp.int32)).astype(jnp.float32)
+
+    tables = (
+        pick(0, number),
+        pick(0, places[0]),
+        pick(0, places[1]),
+        pick(1, rank_of[0]),
+        pick(1, places[0]),
+        jnp.concatenate([kept(0), kept(1)]),
+        last_of(0, user_tiles),
+        last_of(1, item_tiles),
     )
     half = users_share // 2
     users = jnp.concatenate([user_factors[:half], user_factors[half:]], axis=1)
@@ -579,10 +585,10 @@
         pltpu.VMEM((n_row, items_share, vecs), bf16),
         pltpu.VMEM((user_tiles, tile, 2 * rank), bf16),
         pltpu.VMEM((item_tiles, tile, 2 * rank), bf16),
-        pltpu.VMEM((slots + 1, tile, tile), bf16),
-        pltpu.VMEM((slots + 1, tile, tile), bf16),
-        pltpu.VMEM((users_block, items_block), bf16),
-        pltpu.VMEM((items_block, users_block), bf16),
+        pltpu.VMEM((slots, tile, tile), bf16),
+        pltpu.VMEM((slots, tile, tile), bf16),
+        pltpu.VMEM((max(user_tiles, item_tiles), tile, vecs), bf16),
+        pltpu.VMEM((slots + 2, tile, vecs), f32),
         pltpu.VMEM((vecs, vecs), f32),
     ]
     scratch += gather_sems(n_col) + gather_sems(n_row) + gather_sems(n_row)
@@ -610,13 +616,13 @@
             jax.ShapeDtypeStruct((users_share, vecs), f32),
             jax.ShapeDtypeStruct((items_share, vecs), f32),
         ),
-        in_specs=[smem] * 3 + [vmem] * 4,
+        in_specs=[smem] * len(tables) + [vmem] * 4,
         out_specs=(vmem, vmem),
         scratch_shapes=scratch,
         compiler_params=pltpu.CompilerParams(
             collective_id=0, has_side_effects=True, vmem_limit_bytes=62 * 1024 * 1024
         ),
-    )(rows, cols, slot_of, users, items, start_vectors, ratings[0, 0])
+    )(*tables, users, items, start_vectors, ratings[0, 0])
     users_total = users_share * n_row * n_col
     items_total = items_share * n_row * n_col
     return (

time: 194 us -> 179 us (0.923)
  Pallas kernels: 184 us -> 166 us
  other arithmetic: 6.22 us -> 9.4 us
    pallas_call x1, Pallas kernels: 184 us -> 166 us  [shards(): pl.pallas_call(functools.partial(kernel, n_row, n_col), out_shape=(jax.Sh...]
where the time goes in v5:
time: 179 us
  Pallas kernels  166 us (93%)
  other arithmetic  9.4 us (5%)
  local copies, waits for them, and re-layouts  1.97 us (1%)
    pallas_call x1, Pallas kernels, shards(): pl.pallas_call(functools.partial(kernel, n_row, n_col), out_shape=(jax.Sh...  166 us

profile of v5, /device:TPU:0, one launch (start us, length us, event | category | flops | bytes accessed | tf_op | source)
XLA Modules:
  0.0 178.8 jit_solution(14529301425901222508)
XLA Ops:
  1.3 0.7 iota_add_fusion
  2.0 0.2 convert_reduce_fusion
  2.2 0.1 convert_reduce_fusion.3
  2.3 0.5 compare_select_fusion.refs_7_
  2.8 0.2 fusion.2
  3.0 0.1 convert_reduce_fusion.1
  3.1 0.6 compare_select_fusion.1.refs_6_
  3.7 1.5 select_reduce_fusion.1
  5.2 0.7 pad_maximum_fusion.2.refs_5_
  5.9 0.8 fusion.4
  6.7 0.1 copy.17
  6.8 0.1 copy.18
  6.9 0.7 pad_maximum_fusion.1.refs_8_
  7.6 1.0 copy.15
  8.6 0.8 pad_maximum_fusion.refs_9_
  9.4 166.0 %shard_map.86 = (f32[512,128]{1,0:T(8,128)}, f32[512,128]{1,0:T(8,128)}) custom-call(s32[96]{0:T(128)} %get-tuple-element.14.refs_0_, s32[96]{0:T(128)} %get-tuple-element.10.refs_1_, s32[96]{0:T(128)} %get-tuple-element.9.refs_2_, s32[96]{0:T(128)} %get-tuple-element.13.refs_3_, s32[96]{0:T(128)} %get-tuple-element.11.refs_4_, ...), custom_call_target="tpu_custom_call" | custom-call | tf_op jit(solution)/shard_map/pallas_call | solution.py:613
  175.4 1.7 broadcast_multiply_fusion.1
  177.1 1.7 broadcast_multiply_fusion
  (8 shorter events, 0.0 us)

commit v6 on v5

--- a/solution.py
+++ b/solution.py
@@ -1,4 +1,5 @@
 import functools
+import math
 
 import jax
 import jax.numpy as jnp
@@ -10,7 +11,7 @@
 MESH = pl.DeviceIdType.MESH
 HIGHEST = lax.Precision.HIGHEST
 ITERS = 2
-UNROLL = 4
+UNROLL = 8
 TILE = 128
 PANEL = 32
 SUB = 8
@@ -338,10 +339,10 @@
         del refs[:count]
         return got
 
-    slot_of, row_of, col_of, from_slot, back_row, keep, user_last, item_last = take(8)
-    users, items, start, ratings = take(4)
+    slot_of, row_of, col_of, from_slot, back_row, user_keep, item_keep, user_last, item_last = take(9)
+    users, items, start, ratings_far = take(4)
     user_out, item_out = take(2)
-    user_full, item_full, start_full, user_wide, item_wide, res, res_t, basis_tiles, sums_of, work = take(10)
+    user_full, item_full, start_full, user_wide, item_wide, res, res_t, basis_tiles, sums_of, work, ratings, rating_sem = take(12)
     row = Group("row", n_row, "col")
     col = Group("col", n_col, "row")
     user_gather = Gather(col, user_full, take(4))
@@ -355,9 +356,11 @@
     for _ in range(ITERS - 1):
         item_gathers.append(Gather(row, *take(1), take(4)))
     for _ in range(2 * ITERS):
-        grams.append(Gram(row, col, *take(5), take(6)))
+        grams.append(Gram(col, row, *take(5), take(6)))
     assert not refs
 
+    loading = pltpu.make_async_copy(ratings_far, ratings, rating_sem)
+    loading.start()
     barrier = pltpu.get_barrier_semaphore()
     for group in (row, col):
         for t in range(1, group.size):
@@ -366,9 +369,10 @@
             )
     pl.semaphore_wait(barrier, n_row + n_col - 2)
 
-    user_full[col.me] = users[...]
+    half, rank = users.shape[0] // 2, users.shape[1]
+    user_full[col.me] = jnp.concatenate([users[:half, :], users[half:, :]], axis=1)
     user_gather.start()
-    item_full[row.me] = items[...]
+    item_full[row.me] = jnp.concatenate([items[...], items[...]], axis=1)
     item_gather.start()
     start_full[row.me] = start[...]
     start_gather.start()
@@ -379,8 +383,6 @@
     item_gather.finish()
     user_gather.finish()
 
-    half = users.shape[0]
-    rank = users.shape[1] // 2
     piece = min(half, tile)
     low = lax.broadcasted_iota(jnp.int32, (piece, 2 * rank), 1) < rank
 
@@ -399,6 +401,8 @@
     for index in range(n_row):
         for q in range(per_share):
             item_wide[index * per_share + q] = item_full[index, q * tile : (q + 1) * tile, :]
+
+    loading.wait()
 
     def residual(s, _):
         for u in range(UNROLL):
@@ -422,7 +426,7 @@
 
         lax.fori_loop(first, end, some, 0)
 
-    def multiply(matrices, full, pick, way):
+    def multiply(matrices, full, pick, keep):
         for index in range(full.shape[0]):
             per = full.shape[1] // tile
             for q in range(per):
@@ -430,18 +434,18 @@
 
         def some(s, _):
             total = sums_of[slots + 1]
-            for u in range(2 * UNROLL):
-                k = s * 2 * UNROLL + u
+            for u in range(UNROLL):
+                k = s * UNROLL + u
                 part = jnp.dot(
                     matrices[k], basis_tiles[pick[k]], preferred_element_type=jnp.float32
                 )
-                total = part + keep[way * slots + k] * total
+                total = part + keep[k] * total
                 sums_of[k] = total
             sums_of[slots + 1] = total
             return 0
 
         sums_of[slots + 1] = jnp.zeros(sums_of.shape[1:], jnp.float32)
-        lax.fori_loop(0, slots // (2 * UNROLL), some, 0)
+        lax.fori_loop(0, slots // (UNROLL), some, 0)
 
     start_gather.finish()
 
@@ -461,7 +465,7 @@
     for index in range(ITERS):
         last = index == ITERS - 1
         sums, gram, gather = forward_sums[index], grams[2 * index], user_gathers[index]
-        multiply(res, items_now, col_of, 0)
+        multiply(res, items_now, col_of, user_keep)
         sums.send_products(lambda i: sums_of[user_last[i]])
         if index == 0:
             parts = slots // UNROLL // 3
@@ -485,10 +489,10 @@
         gram.collect(work)
         eliminate_from(0)
         if last:
-            user_out[...] = apply(sums)
+            user_out[...] = apply(sums) * math.sqrt(user_out.shape[0] * n_row * n_col)
         gather.arrivals()
         sums, gram = backward_sums[index], grams[2 * index + 1]
-        multiply(res_t, gather.full, back_row, 1)
+        multiply(res_t, gather.full, back_row, item_keep)
         sums.send_products(lambda i: sums_of[item_last[i]])
         sums.pass_on()
         sums.total()
@@ -508,7 +512,7 @@
             gram.spread()
             gram.collect(work)
             eliminate_from(0)
-            item_out[...] = apply(sums)
+            item_out[...] = apply(sums) * math.sqrt(item_out.shape[0] * n_row * n_col)
 
     for part in (
         [user_gather, item_gather, start_gather]
@@ -555,13 +559,12 @@
         pick(0, places[1]),
         pick(1, rank_of[0]),
         pick(1, places[0]),
-        jnp.concatenate([kept(0), kept(1)]),
+        kept(0),
+        kept(1),
         last_of(0, user_tiles),
         last_of(1, item_tiles),
     )
     half = users_share // 2
-    users = jnp.concatenate([user_factors[:half], user_factors[half:]], axis=1)
-    items = jnp.concatenate([item_factors, item_factors], axis=1)
 
     bf16, f32 = jnp.bfloat16, jnp.float32
     dma = pltpu.SemaphoreType.DMA
@@ -590,6 +593,8 @@
         pltpu.VMEM((max(user_tiles, item_tiles), tile, vecs), bf16),
         pltpu.VMEM((slots + 2, tile, vecs), f32),
         pltpu.VMEM((vecs, vecs), f32),
+        pltpu.VMEM((slots, tile, tile), bf16),
+        dma,
     ]
     scratch += gather_sems(n_col) + gather_sems(n_row) + gather_sems(n_row)
     for _ in range(ITERS):
@@ -599,15 +604,15 @@
     for _ in range(ITERS - 1):
         scratch += [pltpu.VMEM((n_row, items_share, vecs), bf16)] + gather_sems(n_row)
     for _ in range(2 * ITERS):
-        part = vecs // n_col
+        part = vecs // n_row
         scratch += [
+            pltpu.VMEM((n_row, part, vecs), f32),
+            pltpu.VMEM((n_row, part, vecs), f32),
+            pltpu.VMEM((1, part, vecs), f32),
             pltpu.VMEM((n_col, part, vecs), f32),
-            pltpu.VMEM((n_col, part, vecs), f32),
-            pltpu.VMEM((1, part, vecs), f32),
             pltpu.VMEM((n_row, part, vecs), f32),
-            pltpu.VMEM((n_col, part, vecs), f32),
         ]
-        scratch += [dma((n_col,)), dma((n_col,)), dma((n_row,)), dma((n_row,)), dma((n_col,)), dma((n_col,))]
+        scratch += [dma((n_row,)), dma((n_row,)), dma((n_col,)), dma((n_col,)), dma((n_row,)), dma((n_row,))]
 
     smem, vmem = pl.BlockSpec(memory_space=pltpu.SMEM), pl.BlockSpec(memory_space=pltpu.VMEM)
     user_basis, item_basis = pl.pallas_call(
@@ -616,19 +621,14 @@
             jax.ShapeDtypeStruct((users_share, vecs), f32),
             jax.ShapeDtypeStruct((items_share, vecs), f32),
         ),
-        in_specs=[smem] * len(tables) + [vmem] * 4,
+        in_specs=[smem] * len(tables) + [vmem] * 3 + [pl.BlockSpec(memory_space=pl.ANY)],
         out_specs=(vmem, vmem),
         scratch_shapes=scratch,
         compiler_params=pltpu.CompilerParams(
             collective_id=0, has_side_effects=True, vmem_limit_bytes=62 * 1024 * 1024
         ),
-    )(*tables, users, items, start_vectors, ratings[0, 0])
-    users_total = users_share * n_row * n_col
-    items_total = items_share * n_row * n_col
-    return (
-        user_basis * jnp.sqrt(jnp.float32(users_total)),
-        item_basis * jnp.sqrt(jnp.float32(items_total)),
-    )
+    )(*tables, user_factors, item_factors, start_vectors, ratings[0, 0])
+    return user_basis, item_basis
 
 
 def solution(mesh):

time: 179 us -> 174 us (0.972)
  Pallas kernels: 166 us -> 161 us
  local copies, waits for them, and re-layouts: 1.97 us -> 6.54 us
  other arithmetic: 9.4 us -> 4.97 us
    unnamed x3 -> x4, local copies, waits for them, and re-layouts: 1.18 us -> 6.53 us
    pallas_call x1, Pallas kernels: 166 us -> 161 us  [shards(): pl.pallas_call(functools.partial(kernel, n_row, n_col), out_shape=(jax.Sh...]
    mul x2 -> x0, other arithmetic: 3.34 us -> none  [the longest x1 1.67 us: shards(): user_basis * jnp.sqrt(jnp.float32(users_total))]
    concatenate x3 -> x0, other arithmetic: 2.17 us -> none  [the longest x1 0.77 us: shards(): items = jnp.concatenate([item_factors, item_factors], axis=1)]
where the time goes in v6:
time: 174 us
  Pallas kernels  161 us (93%)
  local copies, waits for them, and re-layouts  6.54 us (4%)
  other arithmetic  4.97 us (3%)
    pallas_call x1, Pallas kernels, shards(): pl.pallas_call(functools.partial(kernel, n_row, n_col), out_shape=(jax.Sh...  161 us
    unnamed x4, local copies, waits for them, and re-layouts  6.53 us

profile of v6, /device:TPU:0, one launch (start us, length us, event | category | flops | bytes accessed | tf_op | source)
XLA Modules:
  0.0 174.2 jit_solution(11227305163331526686)
XLA Ops:
  1.3 0.7 iota_add_fusion
  2.0 0.2 convert_reduce_fusion
  2.2 0.1 convert_reduce_fusion.1
  2.3 0.5 compare_select_fusion.1.refs_7_
  2.8 0.2 fusion.2
  3.0 0.1 convert_reduce_fusion.3
  3.1 0.5 compare_select_fusion.refs_8_
  3.7 1.5 select_reduce_fusion
  5.1 0.6 convert_element_type.39.refs_6_
  5.7 0.6 convert_element_type.37.refs_5_
  6.3 1.6 copy.11.refs_9_
  7.9 1.6 copy.12.refs_10_
  9.5 161.3 %shard_map.86 = (f32[512,128]{1,0:T(8,128)}, f32[512,128]{1,0:T(8,128)}) custom-call(s32[96]{0:T(128)} %get-tuple-element.10.refs_0_, s32[96]{0:T(128)} %get-tuple-element.7.refs_1_, s32[96]{0:T(128)} %get-tuple-element.5.refs_2_, s32[96]{0:T(128)} %get-tuple-element.9.refs_3_, s32[96]{0:T(128)} %get-tuple-element.8.refs_4_, ...), custom_call_target="tpu_custom_call" | custom-call | tf_op jit(solution)/shard_map/pallas_call | solution.py:618
  170.8 1.7 copy.16
  172.5 1.7 copy.17
  (6 shorter events, 0.0 us)
